TPU v7x, 256 devices: a whole 4x4x8 slice. The times are simulated.
256 devices in a mesh: seq: 32 (over x, y, core), chan: 8 (over z).
Axes of the slice: x: 4, y: 4, z: 8, core: 2. Of those that a mesh axis runs over, the one named last changes fastest.
Arguments:
- query_proj: bfloat16 [16384, 2048], P('seq', 'chan'), may hold values from -6 to 6
- key_proj: bfloat16 [16384, 2048], P('seq', 'chan'), may hold values from -6 to 6
- value_proj: bfloat16 [16384, 2048], P('seq', 'chan'), may hold values from -6 to 6
- short_taps: float32 [3, 3, 2048], P(None, None, 'chan'), may hold values from -1 to 1
- kernel: float32 [16384, 2048], P('seq', 'chan'), may hold values from -1 to 1
- skip: float32 [2048], P('chan'), may hold values from -1 to 1
- out_weight: bfloat16 [2048, 4096], P(None, 'chan'), may hold values from -0.125 to 0.125
Outputs:
- output: bfloat16 [16384, 4096], P('seq', 'chan')
All inputs are finite; a program needn't handle non-finite values.
Results may differ from a plain program's by a relative error of at most 0.005.
Values may be sent and summed in bfloat16 or wider, within the bound.
A program may use at most 64 MiB of HBM per device.

v0:
```python
import functools
import math

import jax
import jax.numpy as jnp
import ml_dtypes
import numpy as np
from jax import lax
from jax.experimental import pallas as pl
from jax.experimental.pallas import tpu as pltpu
from jax.sharding import PartitionSpec as P

LANES = 128
F32 = jnp.float32
BF16 = jnp.bfloat16


def high_low(table):
    high = table.astype(ml_dtypes.bfloat16)
    low = (table - high.astype(np.float64)).astype(ml_dtypes.bfloat16)
    return high, low


def build_tables(outer):
    length = outer * LANES
    position = np.arange(outer)
    lane = np.arange(LANES)
    angle = 2.0 * math.pi / (4 * outer) * ((4 * position[:, None] + 1) * position[None, :] % (4 * outer))
    first = np.concatenate([np.cos(angle), -np.sin(angle)], 0)
    last = np.concatenate([np.cos(angle).T, -np.sin(angle).T], 1) / length
    twist = 2.0 * math.pi / (4 * length) * ((4 * position[:, None] + 1) * lane[None, :] % (4 * length))
    inner = 2.0 * math.pi / LANES * (lane[:, None] * lane[None, :] % LANES)
    cos, sin = np.cos(inner), np.sin(inner)
    forward = np.block([[cos, -sin], [sin, cos]])
    backward = np.block([[cos, sin], [-sin, cos]])
    return (
        np.concatenate(high_low(first), 1),
        np.stack([np.cos(twist), np.sin(twist)]).astype(np.float32),
        np.stack(high_low(forward)),
        np.stack(high_low(backward)),
        np.stack(high_low(last)),
    )


def split(values):
    high = values.astype(BF16)
    return high, (values - high.astype(F32)).astype(BF16)


def dot(lhs, rhs):
    return jnp.dot(lhs, rhs, preferred_element_type=F32)


def operator(
    seq, chan,
    query_hbm, key_hbm, value_hbm, taps_ref, filter_hbm, skip_ref, weight_hbm,
    first_hbm, twist_hbm, forward_hbm, backward_hbm, last_hbm,
    out_ref,
    streams, halo, filt, weight, first, twist, forward, backward, last,
    extended, mixed, gate, stage, send_filter, send_signal, send_conv,
    recv_filter, recv_signal, recv_conv, spectrum, high_ref, low_ref, gathered, total,
    load_sem, halo_sem, send_sem, recv_sem, ring_send, ring_recv,
):
    me = lax.axis_index("seq")
    layer = lax.axis_index("chan")
    tokens = streams.shape[1]
    sub = tokens // LANES
    outer = seq * sub
    groups = streams.shape[2] // LANES
    per = LANES // seq
    block = sub * per
    rows = seq * block

    loads = [
        pltpu.make_async_copy(source, target, load_sem.at[slot])
        for slot, (source, target) in enumerate((
            (filter_hbm, filt),
            (key_hbm, streams.at[1]),
            (value_hbm, streams.at[2]),
            (query_hbm, streams.at[0]),
            (first_hbm, first),
            (twist_hbm, twist),
            (forward_hbm, forward),
            (backward_hbm, backward),
            (last_hbm, last),
            (weight_hbm, weight),
        ))
    ]
    for load in loads:
        load.start()

    barrier = pltpu.get_barrier_semaphore()

    @pl.loop(1, seq)
    def _(step):
        pl.semaphore_signal(barrier, inc=1, device_id={"seq": lax.rem(me + step, seq)})

    right = lax.rem(layer + 1, chan)
    left = lax.rem(layer + chan - 1, chan)
    pl.semaphore_signal(barrier, inc=1, device_id={"chan": right})
    pl.semaphore_signal(barrier, inc=1, device_id={"chan": left})

    def lanes(group):
        return slice(group * LANES, (group + 1) * LANES)

    def scatter(tile, part):
        for channel in range(per):
            stage[pl.ds(part * per + channel, seq, stride=block), :] = tile[channel * seq:(channel + 1) * seq, :]

    def block_of(ref, group, device):
        return ref.at[group, pl.ds(pl.multiple_of(device * block, block), block), :]

    def send_all(source, target, group, slot):
        @pl.loop(1, seq)
        def _(step):
            other = lax.rem(me + step, seq)
            pltpu.make_async_remote_copy(
                src_ref=block_of(source, group, other),
                dst_ref=block_of(target, group, me),
                send_sem=send_sem.at[slot],
                recv_sem=recv_sem.at[slot],
                device_id={"seq": other},
            ).start()

        own = pl.ds(pl.multiple_of(me * block, block), block)
        target[group, own, :] = source[group, own, :]

    def wait_all(ref, group, sem):
        part = ref.at[group, pl.ds(0, (seq - 1) * block), :]
        pltpu.make_async_copy(part, part, sem).wait()

    loads[0].wait()
    for group in range(groups):
        for part in range(sub):
            scatter(filt[part * LANES:(part + 1) * LANES, lanes(group)].T, part)
        send_filter[group] = stage[...].astype(BF16)

    for load in loads[1:4]:
        load.wait()
    pl.semaphore_wait(barrier, seq + 1)
    edge = pltpu.make_async_remote_copy(
        src_ref=streams.at[:, pl.ds(tokens - 16, 16), :],
        dst_ref=halo,
        send_sem=halo_sem.at[0],
        recv_sem=halo_sem.at[1],
        device_id={"seq": lax.rem(me + 1, seq)},
    )
    edge.start()
    for group in range(groups):
        send_all(send_filter, recv_filter, group, group)

    for slot in range(3):
        extended[slot, 16:, :] = streams[slot].astype(F32)
    edge.wait()
    keep = jnp.where(me > 0, 1.0, 0.0).astype(F32)
    for slot in range(3):
        extended[slot, :16, :] = halo[slot].astype(F32) * keep

    def short(slot, part, group):
        base = 16 + part * LANES
        at = lanes(group)
        return (
            taps_ref[0, slot:slot + 1, at] * extended[slot, base:base + LANES, at]
            + taps_ref[1, slot:slot + 1, at] * extended[slot, base - 1:base - 1 + LANES, at]
            + taps_ref[2, slot:slot + 1, at] * extended[slot, base - 2:base - 2 + LANES, at]
        )

    for group in range(groups):
        for part in range(sub):
            tile = short(1, part, group) * short(2, part, group)
            mixed[part * LANES:(part + 1) * LANES, lanes(group)] = tile
            scatter(tile.T, part)
        send_signal[group] = stage[...].astype(BF16)
        send_all(send_signal, recv_signal, group, groups + group)

    for group in range(groups):
        for part in range(sub):
            gate[part * LANES:(part + 1) * LANES, lanes(group)] = short(0, part, group)

    for load in loads[4:9]:
        load.wait()

    def transform(ref, group):
        stage[...] = ref[group].astype(F32)
        for pair in range(per // 2):
            values = jnp.concatenate(
                [stage[pl.ds(2 * pair + side, outer, stride=per), :] for side in range(2)], 1
            ).astype(BF16)
            outer_spec = dot(first[...], jnp.concatenate([values, values], 0))
            for side in range(2):
                real, imag = outer_spec[:outer, lanes(side)], outer_spec[outer:, lanes(side)]
                at = slice((2 * pair + side) * outer, (2 * pair + side + 1) * outer)
                high_ref[at, :LANES], low_ref[at, :LANES] = split(real * twist[0] + imag * twist[1])
                high_ref[at, LANES:], low_ref[at, LANES:] = split(imag * twist[0] - real * twist[1])
        return apply(forward)

    def apply(table):
        high, low = high_ref[...], low_ref[...]
        return dot(high, table[0]) + dot(low, table[0]) + dot(high, table[1])

    for group in range(groups):
        wait_all(recv_filter, group, recv_sem.at[group])
        spectrum[group] = transform(recv_filter, group)

    for group in range(groups):
        wait_all(recv_signal, group, recv_sem.at[groups + group])
        signal = transform(recv_signal, group)
        sig_real, sig_imag = signal[:, :LANES], signal[:, LANES:]
        fil_real, fil_imag = spectrum[group, :, :LANES], spectrum[group, :, LANES:]
        high_ref[:, :LANES], low_ref[:, :LANES] = split(sig_real * fil_real - sig_imag * fil_imag)
        high_ref[:, LANES:], low_ref[:, LANES:] = split(sig_real * fil_imag + sig_imag * fil_real)
        back = apply(backward)
        for pair in range(per // 2):
            sides = []
            for side in range(2):
                at = slice((2 * pair + side) * outer, (2 * pair + side + 1) * outer)
                real, imag = back[at, :LANES], back[at, LANES:]
                sides.append(jnp.concatenate(
                    [real * twist[0] - imag * twist[1], imag * twist[0] + real * twist[1]], 0
                ))
            high, low = split(jnp.concatenate(sides, 1))
            conv = dot(last[0], high) + dot(last[0], low) + dot(last[1], high)
            for side in range(2):
                stage[pl.ds(2 * pair + side, outer, stride=per), :] = conv[:, lanes(side)]
        send_conv[group] = stage[...].astype(BF16)
        send_all(send_conv, recv_conv, group, 2 * groups + group)

    half = tokens // 2
    hops = ((chan // 2, chan - 1 - chan // 2), (chan - 1 - chan // 2, chan // 2))

    def hop(direction, step, group, side):
        origin = lax.rem(layer + (chan - step if direction == 0 else step), chan)
        piece = gathered.at[origin, group, pl.ds(side * half, half), :]
        return pltpu.make_async_remote_copy(
            src_ref=piece,
            dst_ref=piece,
            send_sem=ring_send.at[direction, step, group, side],
            recv_sem=ring_recv.at[direction, step, group, side],
            device_id={"chan": right if direction == 0 else left},
        )

    for group in range(groups):
        wait_all(recv_conv, group, recv_sem.at[2 * groups + group])
        stage[...] = recv_conv[group].astype(F32)
        for part in range(sub):
            conv = jnp.concatenate(
                [stage[pl.ds(part * per + channel, seq, stride=block), :] for channel in range(per)], 0
            ).T
            at = slice(part * LANES, (part + 1) * LANES)
            signal = mixed[at, lanes(group)]
            gated = gate[at, lanes(group)] * (conv + skip_ref[:, lanes(group)] * signal)
            gathered[layer, group, at, :] = gated.astype(BF16)
        for side in range(2):
            for direction in range(2):
                if hops[side][direction] > 0:
                    hop(direction, 0, group, side).start()

    loads[9].wait()

    def project(origin, side, begin):
        at = slice(side * half, (side + 1) * half)
        values = jnp.concatenate([gathered[origin, group, at, :] for group in range(groups)], 1)
        depth = groups * LANES
        product = dot(values, weight[pl.ds(pl.multiple_of(origin * depth, depth), depth), :])
        if begin:
            total[at, :] = product
        else:
            total[at, :] += product

    for side in range(2):
        project(layer, side, True)
    for step in range(1, chan // 2 + 1):
        for group in range(groups):
            for side in range(2):
                for direction in range(2):
                    if step <= hops[side][direction]:
                        hop(direction, step - 1, group, side).wait_recv()
                    if step < hops[side][direction]:
                        hop(direction, step, group, side).start()
        for side in range(2):
            for direction in range(2):
                if step <= hops[side][direction]:
                    origin = lax.rem(layer + (chan - step if direction == 0 else step), chan)
                    project(origin, side, False)
    out_ref[...] = total[...].astype(BF16)

    for group in range(groups):
        for slot, ref in enumerate((send_filter, send_signal, send_conv)):
            wait_all(ref, group, send_sem.at[slot * groups + group])
    for group in range(groups):
        for side in range(2):
            for direction in range(2):
                for step in range(hops[side][direction]):
                    hop(direction, step, group, side).wait_send()


def shards(query_proj, key_proj, value_proj, short_taps, kernel, skip, out_weight):
    seq, chan = lax.axis_size("seq"), lax.axis_size("chan")
    tokens, width = query_proj.shape
    groups = width // LANES
    per = LANES // seq
    outer = seq * tokens // LANES
    rows = outer * per
    features = out_weight.shape[1]
    tables = build_tables(outer)
    anywhere = pl.BlockSpec(memory_space=pl.ANY)
    inside = pl.BlockSpec(memory_space=pltpu.VMEM)
    exchange = pltpu.VMEM((groups, rows, LANES), BF16)
    return pl.pallas_call(
        functools.partial(operator, seq, chan),
        out_shape=jax.ShapeDtypeStruct((tokens, features), BF16),
        in_specs=[anywhere, anywhere, anywhere, inside, anywhere, inside, anywhere] + [anywhere] * 5,
        out_specs=inside,
        scratch_shapes=[
            pltpu.VMEM((3, tokens, width), BF16),
            pltpu.VMEM((3, 16, width), BF16),
            pltpu.VMEM((tokens, width), F32),
            pltpu.VMEM(out_weight.shape, BF16),
            *(pltpu.VMEM(table.shape, table.dtype) for table in tables),
            pltpu.VMEM((3, tokens + 16, width), F32),
            pltpu.VMEM((tokens, width), F32),
            pltpu.VMEM((tokens, width), F32),
            pltpu.VMEM((rows, LANES), F32),
            exchange, exchange, exchange, exchange, exchange, exchange,
            pltpu.VMEM((groups, rows, 2 * LANES), F32),
            pltpu.VMEM((rows, 2 * LANES), BF16),
            pltpu.VMEM((rows, 2 * LANES), BF16),
            pltpu.VMEM((chan, groups, tokens, LANES), BF16),
            pltpu.VMEM((tokens, features), F32),
            pltpu.SemaphoreType.DMA((10,)),
            pltpu.SemaphoreType.DMA((2,)),
            pltpu.SemaphoreType.DMA((3 * groups,)),
            pltpu.SemaphoreType.DMA((3 * groups,)),
            pltpu.SemaphoreType.DMA((2, max(1, chan // 2), groups, 2)),
            pltpu.SemaphoreType.DMA((2, max(1, chan // 2), groups, 2)),
        ],
        compiler_params=pltpu.CompilerParams(
            collective_id=0, has_side_effects=True, vmem_limit_bytes=56 * 1024 * 1024
        ),
        cost_estimate=pl.CostEstimate(flops=2_000_000_000, bytes_accessed=5_000_000, transcendentals=0),
    )(
        query_proj, key_proj, value_proj, short_taps, kernel, skip.reshape(1, width), out_weight,
        *(jnp.asarray(table) for table in tables),
    )


def solution(mesh):
    return jax.shard_map(
        shards,
        mesh=mesh,
        in_specs=(
            P("seq", "chan"),
            P("seq", "chan"),
            P("seq", "chan"),
            P(None, None, "chan"),
            P("seq", "chan"),
            P("chan"),
            P(None, "chan"),
        ),
        out_specs=P("seq", "chan"),
        check_vma=False,
    )
```

profile of v0, /device:TPU:1, one launch (start us, length us, event | category | flops | bytes accessed | tf_op | source)
XLA Modules:
  0.0 52.7 jit_solution(2190283622399765499)
XLA Ops:
  0.0 50.8 %shard_map.118 = bf16[512,512]{1,0:T(8,128)(2,1)} custom-call(bf16[512,256]{1,0:T(8,128)(2,1)} %query_hbm.1, bf16[512,256]{1,0:T(8,128)(2,1)} %key_hbm.1, bf16[512,256]{1,0:T(8,128)(2,1)} %value_hbm.1, f32[3,3,256]{2,1,0:T(4,128)} %taps_ref.1, f32[512,256]{1,0:T(8,128)} %filter_hbm.1, f32[1,256]{1,0:T(1,128)} %bitcast.1, bf16[2048,512]{1,0:T(8,128)(2,1)} %weight_hbm.1, ...), custom_call_target="tpu_custom_call" | custom-call | flops 2000000000 | bytes 5000000 | tf_op jit(solution)/shard_map/pallas_call | solution.py:309
  50.8 1.9 %copy.14 = bf16[512,512]{1,0:T(8,128)(2,1)} copy(bf16[512,512]{1,0:T(8,128)(2,1)} %shard_map.118) | data formatting | bytes 1048576
where the time goes:
time: 52.9 us; the launch traced here: 52.7 us
  Pallas kernels  50.8 us (96%)
  local copies, waits for them, and re-layouts  1.87 us (4%)
    pallas_call x1, Pallas kernels, shards(): pl.pallas_call(functools.partial(operator, seq, chan), out_shape=jax.Shap...  50.8 us
    unnamed x1, local copies, waits for them, and re-layouts  1.87 us

commit v1 on v0

--- a/solution.py
+++ b/solution.py
@@ -13,6 +13,7 @@
 LANES = 128
 F32 = jnp.float32
 BF16 = jnp.bfloat16
+GRIDS = {32: (4, 4, 2), 8: (2, 2, 2), 4: (1, 2, 2)}
 
 
 def high_low(table):
@@ -51,12 +52,23 @@
     return jnp.dot(lhs, rhs, preferred_element_type=F32)
 
 
+def peers(me, grid):
+    along_x, along_y, cores = grid
+    x, y, core = me // (along_y * cores), me // cores % along_y, me % cores
+    steps = [(i, j, k) for i in range(along_x) for j in range(along_y) for k in range(cores)][1:]
+    steps.sort(key=lambda step: -4 * (min(step[0], along_x - step[0]) + min(step[1], along_y - step[1])) - step[2])
+    return [
+        ((x + i) % along_x * along_y + (y + j) % along_y) * cores + (core + k) % cores
+        for i, j, k in steps
+    ]
+
+
 def operator(
-    seq, chan,
-    query_hbm, key_hbm, value_hbm, taps_ref, filter_hbm, skip_ref, weight_hbm,
+    grid, seq, chan,
+    query_hbm, key_hbm, value_hbm, taps_hbm, filter_hbm, skip_hbm, weight_hbm,
     first_hbm, twist_hbm, forward_hbm, backward_hbm, last_hbm,
     out_ref,
-    streams, halo, filt, weight, first, twist, forward, backward, last,
+    streams, halo, filt, taps_ref, skip_ref, weight, first, twist, forward, backward, last,
     extended, mixed, gate, stage, send_filter, send_signal, send_conv,
     recv_filter, recv_signal, recv_conv, spectrum, high_ref, low_ref, gathered, total,
     load_sem, halo_sem, send_sem, recv_sem, ring_send, ring_recv,
@@ -78,6 +90,8 @@
             (key_hbm, streams.at[1]),
             (value_hbm, streams.at[2]),
             (query_hbm, streams.at[0]),
+            (taps_hbm, taps_ref),
+            (skip_hbm, skip_ref),
             (first_hbm, first),
             (twist_hbm, twist),
             (forward_hbm, forward),
@@ -86,19 +100,17 @@
             (weight_hbm, weight),
         ))
     ]
-    for load in loads:
-        load.start()
-
     barrier = pltpu.get_barrier_semaphore()
 
-    @pl.loop(1, seq)
-    def _(step):
-        pl.semaphore_signal(barrier, inc=1, device_id={"seq": lax.rem(me + step, seq)})
-
+    others = peers(me, grid)
+    for other in others:
+        pl.semaphore_signal(barrier, inc=1, device_id={"seq": other})
     right = lax.rem(layer + 1, chan)
     left = lax.rem(layer + chan - 1, chan)
     pl.semaphore_signal(barrier, inc=1, device_id={"chan": right})
     pl.semaphore_signal(barrier, inc=1, device_id={"chan": left})
+    for load in loads:
+        load.start()
 
     def lanes(group):
         return slice(group * LANES, (group + 1) * LANES)
@@ -111,9 +123,7 @@
         return ref.at[group, pl.ds(pl.multiple_of(device * block, block), block), :]
 
     def send_all(source, target, group, slot):
-        @pl.loop(1, seq)
-        def _(step):
-            other = lax.rem(me + step, seq)
+        for other in others:
             pltpu.make_async_remote_copy(
                 src_ref=block_of(source, group, other),
                 dst_ref=block_of(target, group, me),
@@ -135,7 +145,7 @@
             scatter(filt[part * LANES:(part + 1) * LANES, lanes(group)].T, part)
         send_filter[group] = stage[...].astype(BF16)
 
-    for load in loads[1:4]:
+    for load in loads[1:6]:
         load.wait()
     pl.semaphore_wait(barrier, seq + 1)
     edge = pltpu.make_async_remote_copy(
@@ -177,7 +187,7 @@
         for part in range(sub):
             gate[part * LANES:(part + 1) * LANES, lanes(group)] = short(0, part, group)
 
-    for load in loads[4:9]:
+    for load in loads[6:11]:
         load.wait()
 
     def transform(ref, group):
@@ -226,7 +236,7 @@
         send_all(send_conv, recv_conv, group, 2 * groups + group)
 
     half = tokens // 2
-    hops = ((chan // 2, chan - 1 - chan // 2), (chan - 1 - chan // 2, chan // 2))
+    hops = ((chan - 1) // 2, chan // 2)
 
     def hop(direction, step, group, side):
         origin = lax.rem(layer + (chan - step if direction == 0 else step), chan)
@@ -252,45 +262,47 @@
             gathered[layer, group, at, :] = gated.astype(BF16)
         for side in range(2):
             for direction in range(2):
-                if hops[side][direction] > 0:
+                if hops[direction] > 0:
                     hop(direction, 0, group, side).start()
 
-    loads[9].wait()
-
-    def project(origin, side, begin):
+    loads[11].wait()
+
+    def product(origin, side):
         at = slice(side * half, (side + 1) * half)
         values = jnp.concatenate([gathered[origin, group, at, :] for group in range(groups)], 1)
         depth = groups * LANES
-        product = dot(values, weight[pl.ds(pl.multiple_of(origin * depth, depth), depth), :])
-        if begin:
-            total[at, :] = product
-        else:
-            total[at, :] += product
+        return dot(values, weight[pl.ds(pl.multiple_of(origin * depth, depth), depth), :])
 
     for side in range(2):
-        project(layer, side, True)
+        total[side * half:(side + 1) * half, :] = product(layer, side)
     for step in range(1, chan // 2 + 1):
-        for group in range(groups):
+        final = step == chan // 2
+        for direction in (1, 0):
+            if step > hops[direction]:
+                continue
+            origin = lax.rem(layer + (chan - step if direction == 0 else step), chan)
             for side in range(2):
-                for direction in range(2):
-                    if step <= hops[side][direction]:
-                        hop(direction, step - 1, group, side).wait_recv()
-                    if step < hops[side][direction]:
+                at = slice(side * half, (side + 1) * half)
+                for group in range(groups):
+                    hop(direction, step - 1, group, side).wait_recv()
+                    if step < hops[direction]:
                         hop(direction, step, group, side).start()
+                if final:
+                    out_ref[at, :] = (total[at, :] + product(origin, side)).astype(BF16)
+        if not final:
+            for direction in (1, 0):
+                if step <= hops[direction]:
+                    origin = lax.rem(layer + (chan - step if direction == 0 else step), chan)
+                    for side in range(2):
+                        total[side * half:(side + 1) * half, :] += product(origin, side)
+
+    for group in range(groups):
+        for slot, ref in enumerate((send_filter, send_signal, send_conv)):
+            wait_all(ref, group, send_sem.at[slot * groups + group])
+    for group in range(groups):
         for side in range(2):
             for direction in range(2):
-                if step <= hops[side][direction]:
-                    origin = lax.rem(layer + (chan - step if direction == 0 else step), chan)
-                    project(origin, side, False)
-    out_ref[...] = total[...].astype(BF16)
-
-    for group in range(groups):
-        for slot, ref in enumerate((send_filter, send_signal, send_conv)):
-            wait_all(ref, group, send_sem.at[slot * groups + group])
-    for group in range(groups):
-        for side in range(2):
-            for direction in range(2):
-                for step in range(hops[side][direction]):
+                for step in range(hops[direction]):
                     hop(direction, step, group, side).wait_send()
 
 
@@ -307,14 +319,16 @@
     inside = pl.BlockSpec(memory_space=pltpu.VMEM)
     exchange = pltpu.VMEM((groups, rows, LANES), BF16)
     return pl.pallas_call(
-        functools.partial(operator, seq, chan),
-        out_shape=jax.ShapeDtypeStruct((tokens, features), BF16),
-        in_specs=[anywhere, anywhere, anywhere, inside, anywhere, inside, anywhere] + [anywhere] * 5,
+        functools.partial(operator, GRIDS[seq], seq, chan),
+        out_shape=pltpu.VMEM((tokens, features), BF16),
+        in_specs=[anywhere] * 12,
         out_specs=inside,
         scratch_shapes=[
             pltpu.VMEM((3, tokens, width), BF16),
             pltpu.VMEM((3, 16, width), BF16),
             pltpu.VMEM((tokens, width), F32),
+            pltpu.VMEM(short_taps.shape, F32),
+            pltpu.VMEM((1, width), F32),
             pltpu.VMEM(out_weight.shape, BF16),
             *(pltpu.VMEM(table.shape, table.dtype) for table in tables),
             pltpu.VMEM((3, tokens + 16, width), F32),
@@ -327,7 +341,7 @@
             pltpu.VMEM((rows, 2 * LANES), BF16),
             pltpu.VMEM((chan, groups, tokens, LANES), BF16),
             pltpu.VMEM((tokens, features), F32),
-            pltpu.SemaphoreType.DMA((10,)),
+            pltpu.SemaphoreType.DMA((12,)),
             pltpu.SemaphoreType.DMA((2,)),
             pltpu.SemaphoreType.DMA((3 * groups,)),
             pltpu.SemaphoreType.DMA((3 * groups,)),

time: 52.9 us -> 48.7 us (0.921)
  Pallas kernels: 50.8 us -> 47.5 us
  local copies, waits for them, and re-layouts: 1.87 us -> 0.8 us
    pallas_call x1, Pallas kernels: 50.8 us -> 47.5 us  [shards(): pl.pallas_call(functools.partial(operator, GRIDS[seq], seq, chan), out_sh...]
    unnamed x1, local copies, waits for them, and re-layouts: 1.87 us -> 0.8 us
where the time goes in v1:
time: 48.7 us; the launch traced here: 48.3 us
  Pallas kernels  47.5 us (98%)
  local copies, waits for them, and re-layouts  0.8 us (2%)
    pallas_call x1, Pallas kernels, shards(): pl.pallas_call(functools.partial(operator, GRIDS[seq], seq, chan), out_sh...  47.5 us

profile of v1, /device:TPU:1, one launch (start us, length us, event | category | flops | bytes accessed | tf_op | source)
XLA Modules:
  0.0 48.3 jit_solution(14406330993445957948)
XLA Ops:
  0.0 47.5 %shard_map.118 = bf16[512,512]{1,0:T(8,128)(2,1)S(1)} custom-call(bf16[512,256]{1,0:T(8,128)(2,1)} %query_hbm.1, bf16[512,256]{1,0:T(8,128)(2,1)} %key_hbm.1, bf16[512,256]{1,0:T(8,128)(2,1)} %value_hbm.1, f32[3,3,256]{2,1,0:T(4,128)} %taps_hbm.1, f32[512,256]{1,0:T(8,128)} %filter_hbm.1, f32[1,256]{1,0:T(1,128)} %bitcast.1, bf16[2048,512]{1,0:T(8,128)(2,1)} %weight_hbm.1, ...), custom_call_target="tpu_custom_call" | custom-call | flops 2000000000 | bytes 5000000 | tf_op jit(solution)/shard_map/pallas_call | solution.py:321
  47.5 0.8 %copy.14 = bf16[512,512]{1,0:T(8,128)(2,1)} copy(bf16[512,512]{1,0:T(8,128)(2,1)S(1)} %shard_map.118) | data formatting | bytes 1048576

commit v2 on v1

v2 whole, which is shorter than its diff:
```python
import functools
import math

import jax
import jax.numpy as jnp
import ml_dtypes
import numpy as np
from jax import lax
from jax.experimental import pallas as pl
from jax.experimental.pallas import tpu as pltpu
from jax.sharding import PartitionSpec as P

LANES = 128
F32 = jnp.float32
BF16 = jnp.bfloat16
RIGHTWARD, LEFTWARD_LAYER = (0,), 0
GRIDS = {32: (4, 4, 2), 8: (2, 2, 2), 4: (1, 2, 2)}


def high_low(table):
    high = table.astype(ml_dtypes.bfloat16)
    low = (table - high.astype(np.float64)).astype(ml_dtypes.bfloat16)
    return high, low


def build_tables(outer):
    length = outer * LANES
    position = np.arange(outer)
    lane = np.arange(LANES)
    angle = 2.0 * math.pi / (4 * outer) * ((4 * position[:, None] + 1) * position[None, :] % (4 * outer))
    first = np.concatenate([np.cos(angle), -np.sin(angle)], 0)
    last = np.concatenate([np.cos(angle).T, -np.sin(angle).T], 1) / length
    twist = 2.0 * math.pi / (4 * length) * ((4 * position[:, None] + 1) * lane[None, :] % (4 * length))
    inner = 2.0 * math.pi / LANES * (lane[:, None] * lane[None, :] % LANES)
    cos, sin = np.cos(inner), np.sin(inner)
    forward = np.block([[cos, -sin], [sin, cos]])
    backward = np.block([[cos, sin], [-sin, cos]])
    return (
        np.concatenate(high_low(first), 1),
        np.stack([np.cos(twist), np.sin(twist)]).astype(np.float32),
        np.stack(high_low(forward)),
        np.stack(high_low(backward)),
        np.stack(high_low(last)),
    )


def split(values):
    high = values.astype(BF16)
    return high, (values - high.astype(F32)).astype(BF16)


def dot(lhs, rhs):
    return jnp.dot(lhs, rhs, preferred_element_type=F32)


def peers(me, grid):
    along_x, along_y, cores = grid
    x, y, core = me // (along_y * cores), me // cores % along_y, me % cores
    steps = [(i, j, k) for i in range(along_x) for j in range(along_y) for k in range(cores)][1:]
    steps.sort(key=lambda step: -4 * (min(step[0], along_x - step[0]) + min(step[1], along_y - step[1])) - step[2])
    return [
        ((x + i) % along_x * along_y + (y + j) % along_y) * cores + (core + k) % cores
        for i, j, k in steps
    ]


def operator(
    grid, seq, chan,
    query_hbm, key_hbm, value_hbm, taps_hbm, filter_hbm, skip_hbm, weight_hbm,
    first_hbm, twist_hbm, forward_hbm, backward_hbm, last_hbm,
    out_ref,
    streams, halo, filt, taps_ref, skip_ref, weight, first, twist, forward, backward, last,
    extended, mixed, gate, stage, edges, send_edge, recv_edge, send_in, recv_in, send_conv, recv_conv,
    spectrum, high_ref, low_ref, gathered, total,
    load_sem, halo_sem, send_sem, recv_sem, ring_send, ring_recv,
):
    me = lax.axis_index("seq")
    layer = lax.axis_index("chan")
    tokens = streams.shape[1]
    sub = tokens // LANES
    outer = seq * sub
    width = streams.shape[2]
    groups = width // LANES
    per = LANES // seq
    block = sub * per
    rows = seq * block

    loads = [
        pltpu.make_async_copy(source, target, load_sem.at[slot])
        for slot, (source, target) in enumerate((
            (filter_hbm, filt),
            (key_hbm, streams.at[1]),
            (value_hbm, streams.at[2]),
            (query_hbm, streams.at[0]),
            (taps_hbm, taps_ref),
            (skip_hbm, skip_ref),
            (first_hbm, first),
            (twist_hbm, twist),
            (forward_hbm, forward),
            (backward_hbm, backward),
            (last_hbm, last),
            (weight_hbm, weight),
        ))
    ]
    barrier = pltpu.get_barrier_semaphore()

    others = peers(me, grid)
    for other in others:
        pl.semaphore_signal(barrier, inc=1, device_id={"seq": other})
    right = lax.rem(layer + 1, chan)
    left = lax.rem(layer + chan - 1, chan)
    pl.semaphore_signal(barrier, inc=1, device_id={"chan": right})
    pl.semaphore_signal(barrier, inc=1, device_id={"chan": left})
    for load in loads:
        load.start()

    def lanes(group):
        return slice(group * LANES, (group + 1) * LANES)

    def scatter(tile, part):
        for channel in range(per):
            stage[pl.ds(part * per + channel, seq, stride=block), :] = tile[channel * seq:(channel + 1) * seq, :]

    def staged():
        return stage[...].astype(BF16).reshape(seq, block, LANES)

    def send_all(source, target, slot):
        for other in others:
            pltpu.make_async_remote_copy(
                src_ref=source.at[other],
                dst_ref=target.at[me],
                send_sem=send_sem.at[slot],
                recv_sem=recv_sem.at[slot],
                device_id={"seq": other},
            ).start()
        target[me] = source[me]

    def wait_all(ref, sem):
        part = ref.at[pl.ds(0, seq - 1)]
        pltpu.make_async_copy(part, part, sem).wait()

    def short(slot, group, base=0, count=LANES):
        at = lanes(group)
        base += 16
        return (
            taps_ref[0, slot:slot + 1, at] * extended[slot, base:base + count, at]
            + taps_ref[1, slot:slot + 1, at] * extended[slot, base - 1:base - 1 + count, at]
            + taps_ref[2, slot:slot + 1, at] * extended[slot, base - 2:base - 2 + count, at]
        )

    def prepare(group):
        for part in range(sub):
            scatter(filt[part * LANES:(part + 1) * LANES, lanes(group)].T, part)
        send_in[group, 0] = staged()
        for part in range(sub):
            tile = short(1, group, part * LANES) * short(2, group, part * LANES)
            mixed[part * LANES:(part + 1) * LANES, lanes(group)] = tile
            scatter(tile.T, part)
        send_in[group, 1] = staged()

    loads[4].wait()
    for slot in (1, 2):
        loads[slot].wait()
        extended[slot, 8:16, :] = jnp.zeros((8, width), F32)
        extended[slot, 16:, :] = streams[slot].astype(F32)

    parts = []
    for begin in (True, False):
        for slot in (1, 2):
            tap = [taps_ref[shift, slot:slot + 1, :] for shift in range(3)]
            if begin:
                head = [extended[slot, 16 + row:17 + row, :] for row in range(2)]
                parts += [tap[0] * head[0], tap[0] * head[1] + tap[1] * head[0]]
            else:
                tail = [extended[slot, 14 + tokens + row:15 + tokens + row, :] for row in range(2)]
                parts += [tap[1] * tail[1] + tap[2] * tail[0], tap[2] * tail[1]]
    parts = jnp.concatenate(parts, 0)
    edges[...] = jnp.zeros(edges.shape, F32)
    for group in range(groups):
        for channel in range(per):
            at = (group * per + channel) * 8
            edges[at:at + 8, :] = pltpu.roll(parts[:, lanes(group)], (LANES - channel * seq) % LANES, 1)
    by_holder = edges[...].T
    for holder in range(seq):
        send_edge[holder] = by_holder[holder:holder + 1, :]

    loads[0].wait()
    prepare(0)
    pl.semaphore_wait(barrier, seq + 1)
    for which in range(2):
        send_all(send_in.at[0, which], recv_in.at[0, which], which)
    send_all(send_edge, recv_edge, 2 * groups)
    for group in range(1, groups):
        prepare(group)
        for which in range(2):
            send_all(send_in.at[group, which], recv_in.at[group, which], 2 * group + which)
    loads[3].wait()
    edge = pltpu.make_async_remote_copy(
        src_ref=streams.at[:, pl.ds(tokens - 16, 16), :],
        dst_ref=halo,
        send_sem=halo_sem.at[0],
        recv_sem=halo_sem.at[1],
        device_id={"seq": lax.rem(me + 1, seq)},
    )
    edge.start()
    extended[0, 16:, :] = streams[0].astype(F32)
    for load in loads[5:11]:
        load.wait()

    def apply(table):
        high, low = high_ref[...], low_ref[...]
        return dot(high, table[0]) + dot(low, table[0]) + dot(high, table[1])

    def transform(group, which):
        stage[...] = recv_in[group, which].reshape(rows, LANES).astype(F32)
        if which == 1:
            first_lanes = lax.broadcasted_iota(jnp.int32, (seq, LANES), 1) < 2
            for channel in range(per):
                at = pl.ds(channel, seq, stride=block)
                place = (group * per + channel) * 8
                whole = pltpu.roll(heads, (wide - place) % wide, 1)[:, :LANES]
                stage[at, :] = jnp.where(first_lanes, whole, stage[at, :])
        for pair in range(per // 2):
            values = jnp.concatenate(
                [stage[pl.ds(2 * pair + side, outer, stride=per), :] for side in range(2)], 1
            ).astype(BF16)
            outer_spec = dot(first[...], jnp.concatenate([values, values], 0))
            for side in range(2):
                real, imag = outer_spec[:outer, lanes(side)], outer_spec[outer:, lanes(side)]
                at = slice((2 * pair + side) * outer, (2 * pair + side + 1) * outer)
                high_ref[at, :LANES], low_ref[at, :LANES] = split(real * twist[0] + imag * twist[1])
                high_ref[at, LANES:], low_ref[at, LANES:] = split(imag * twist[0] - real * twist[1])
        spectrum[which * rows:(which + 1) * rows, :] = apply(forward)

    for group in range(groups):
        wait_all(recv_in.at[group, 0], recv_sem.at[2 * group])
        transform(group, 0)
        wait_all(recv_in.at[group, 1], recv_sem.at[2 * group + 1])
        if group == 0:
            wait_all(recv_edge, recv_sem.at[2 * groups])
            own = jnp.concatenate([recv_edge[holder] for holder in range(seq)], 0)
            wide = own.shape[1]
            first_row = lax.broadcasted_iota(jnp.int32, own.shape, 0) < 1
            carried = jnp.where(first_row, 0.0, pltpu.roll(own, 1, 0))
            short_heads = own + pltpu.roll(carried, wide - 4, 1)
            heads = short_heads * pltpu.roll(short_heads, wide - 2, 1)
        transform(group, 1)
        fil_real, fil_imag = spectrum[:rows, :LANES], spectrum[:rows, LANES:]
        sig_real, sig_imag = spectrum[rows:, :LANES], spectrum[rows:, LANES:]
        high_ref[:, :LANES], low_ref[:, :LANES] = split(sig_real * fil_real - sig_imag * fil_imag)
        high_ref[:, LANES:], low_ref[:, LANES:] = split(sig_real * fil_imag + sig_imag * fil_real)
        back = apply(backward)
        for pair in range(per // 2):
            sides = []
            for side in range(2):
                at = slice((2 * pair + side) * outer, (2 * pair + side + 1) * outer)
                real, imag = back[at, :LANES], back[at, LANES:]
                sides.append(jnp.concatenate(
                    [real * twist[0] - imag * twist[1], imag * twist[0] + real * twist[1]], 0
                ))
            high, low = split(jnp.concatenate(sides, 1))
            conv = dot(last[0], high) + dot(last[0], low) + dot(last[1], high)
            for side in range(2):
                stage[pl.ds(2 * pair + side, outer, stride=per), :] = conv[:, lanes(side)]
        send_conv[group] = staged()
        send_all(send_conv.at[group], recv_conv.at[group], 2 * groups + 1 + group)

    edge.wait()
    keep = jnp.where(me > 0, 1.0, 0.0).astype(F32)
    for slot in range(3):
        extended[slot, :16, :] = halo[slot].astype(F32) * keep
    for group in range(groups):
        mixed[:8, lanes(group)] = short(1, group, 0, 8) * short(2, group, 0, 8)
        for part in range(sub):
            gate[part * LANES:(part + 1) * LANES, lanes(group)] = short(0, group, part * LANES)

    farthest = chan // 2

    def hop(direction, step, group):
        origin = lax.rem(layer + (chan - step if direction == 0 else step), chan)
        piece = gathered.at[origin, group]
        return pltpu.make_async_remote_copy(
            src_ref=piece,
            dst_ref=piece,
            send_sem=ring_send.at[direction, step, group],
            recv_sem=ring_recv.at[direction, step, group],
            device_id={"chan": right if direction == 0 else left},
        )

    def if_used(direction, step, group, target, act):
        if step < farthest - 1:
            act()
        elif group in RIGHTWARD:
            pl.when(target != LEFTWARD_LAYER if direction == 0 else target == LEFTWARD_LAYER)(act)
        elif direction == 1:
            act()

    def pass_on(direction, step, group):
        if_used(direction, step, group, right if direction == 0 else left, lambda: hop(direction, step, group).start())

    for group in range(groups):
        wait_all(recv_conv.at[group], recv_sem.at[2 * groups + 1 + group])
        stage[...] = recv_conv[group].reshape(rows, LANES).astype(F32)
        for part in range(sub):
            conv = jnp.concatenate(
                [stage[pl.ds(part * per + channel, seq, stride=block), :] for channel in range(per)], 0
            ).T
            at = slice(part * LANES, (part + 1) * LANES)
            signal = mixed[at, lanes(group)]
            gated = gate[at, lanes(group)] * (conv + skip_ref[:, lanes(group)] * signal)
            gathered[layer, group, at, :] = gated.astype(BF16)
        for direction in (1, 0):
            pass_on(direction, 0, group)

    loads[11].wait()

    def product(origin, begin, count, members=tuple(range(groups))):
        values = jnp.concatenate([gathered[origin, group, begin:begin + count, :] for group in members], 1)
        depth = groups * LANES
        at = pl.ds(pl.multiple_of(origin * depth + members[0] * LANES, LANES), len(members) * LANES)
        return dot(values, weight[at, :])

    def origin_of(direction, step):
        return lax.rem(layer + (chan - step if direction == 0 else step), chan)

    half = tokens // 2
    for begin in (0, half):
        total[begin:begin + half, :] = product(layer, begin, half)
    for step in range(1, farthest + 1):
        for group in range(groups):
            for direction in (1, 0):
                if_used(direction, step - 1, group, layer, lambda: hop(direction, step - 1, group).wait_recv())
                if step < farthest:
                    pass_on(direction, step, group)
            if step == farthest:
                for begin in (0, half):
                    at = slice(begin, begin + half)
                    value = total[at, :] + product(origin_of(1, step), begin, half, (group,))
                    if group < groups - 1:
                        total[at, :] = value
                    else:
                        out_ref[at, :] = value.astype(BF16)
        if step < farthest:
            for direction in (1, 0):
                for begin in (0, half):
                    total[begin:begin + half, :] += product(origin_of(direction, step), begin, half)

    wait_all(send_edge, send_sem.at[2 * groups])
    for group in range(groups):
        for which in range(2):
            wait_all(send_in.at[group, which], send_sem.at[2 * group + which])
        wait_all(send_conv.at[group], send_sem.at[2 * groups + 1 + group])
        for direction in range(2):
            for step in range(farthest):
                if_used(
                    direction, step, group, right if direction == 0 else left,
                    lambda: hop(direction, step, group).wait_send(),
                )


def shards(query_proj, key_proj, value_proj, short_taps, kernel, skip, out_weight):
    seq, chan = lax.axis_size("seq"), lax.axis_size("chan")
    tokens, width = query_proj.shape
    groups = width // LANES
    per = LANES // seq
    outer = seq * tokens // LANES
    rows = outer * per
    features = out_weight.shape[1]
    tables = build_tables(outer)
    anywhere = pl.BlockSpec(memory_space=pl.ANY)
    inside = pl.BlockSpec(memory_space=pltpu.VMEM)
    block = rows // seq
    wide = -(-groups * per * 8 // LANES) * LANES
    incoming = pltpu.VMEM((groups, 2, seq, block, LANES), BF16)
    returned = pltpu.VMEM((groups, seq, block, LANES), BF16)
    edge = pltpu.VMEM((seq, 1, wide), F32)
    return pl.pallas_call(
        functools.partial(operator, GRIDS[seq], seq, chan),
        out_shape=pltpu.VMEM((tokens, features), BF16),
        in_specs=[anywhere] * 12,
        out_specs=inside,
        scratch_shapes=[
            pltpu.VMEM((3, tokens, width), BF16),
            pltpu.VMEM((3, 16, width), BF16),
            pltpu.VMEM((tokens, width), F32),
            pltpu.VMEM(short_taps.shape, F32),
            pltpu.VMEM((1, width), F32),
            pltpu.VMEM(out_weight.shape, BF16),
            *(pltpu.VMEM(table.shape, table.dtype) for table in tables),
            pltpu.VMEM((3, tokens + 16, width), F32),
            pltpu.VMEM((tokens, width), F32),
            pltpu.VMEM((tokens, width), F32),
            pltpu.VMEM((rows, LANES), F32),
            pltpu.VMEM((wide, LANES), F32),
            edge, edge, incoming, incoming, returned, returned,
            pltpu.VMEM((2 * rows, 2 * LANES), F32),
            pltpu.VMEM((rows, 2 * LANES), BF16),
            pltpu.VMEM((rows, 2 * LANES), BF16),
            pltpu.VMEM((chan, groups, tokens, LANES), BF16),
            pltpu.VMEM((tokens, features), F32),
            pltpu.SemaphoreType.DMA((12,)),
            pltpu.SemaphoreType.DMA((2,)),
            pltpu.SemaphoreType.DMA((3 * groups + 1,)),
            pltpu.SemaphoreType.DMA((3 * groups + 1,)),
            pltpu.SemaphoreType.DMA((2, max(1, chan // 2), groups)),
            pltpu.SemaphoreType.DMA((2, max(1, chan // 2), groups)),
        ],
        compiler_params=pltpu.CompilerParams(
            collective_id=0, has_side_effects=True, vmem_limit_bytes=56 * 1024 * 1024
        ),
        cost_estimate=pl.CostEstimate(flops=2_000_000_000, bytes_accessed=5_000_000, transcendentals=0),
    )(
        query_proj, key_proj, value_proj, short_taps, kernel, skip.reshape(1, width), out_weight,
        *(jnp.asarray(table) for table in tables),
    )


def solution(mesh):
    return jax.shard_map(
        shards,
        mesh=mesh,
        in_specs=(
            P("seq", "chan"),
            P("seq", "chan"),
            P("seq", "chan"),
            P(None, None, "chan"),
            P("seq", "chan"),
            P("chan"),
            P(None, "chan"),
        ),
        out_specs=P("seq", "chan"),
        check_vma=False,
    )
```

time: 48.7 us -> 47.2 us (0.969)
  the two profiles are of different devices: /device:TPU:1 before, /device:TPU:64 now
where the time goes in v2:
time: 47.2 us; the launch traced here: 47.1 us
  Pallas kernels  46.3 us (98%)
  local copies, waits for them, and re-layouts  0.8 us (2%)
    pallas_call x1, Pallas kernels, shards(): pl.pallas_call(functools.partial(operator, GRIDS[seq], seq, chan), out_sh...  46.3 us

profile of v2, /device:TPU:64, one launch (start us, length us, event | category | flops | bytes accessed | tf_op | source)
XLA Modules:
  0.0 47.1 jit_solution(6662483812613830110)
XLA Ops:
  0.0 46.3 %shard_map.118 = bf16[512,512]{1,0:T(8,128)(2,1)S(1)} custom-call(bf16[512,256]{1,0:T(8,128)(2,1)} %query_hbm.1, bf16[512,256]{1,0:T(8,128)(2,1)} %key_hbm.1, bf16[512,256]{1,0:T(8,128)(2,1)} %value_hbm.1, f32[3,3,256]{2,1,0:T(4,128)} %taps_hbm.1, f32[512,256]{1,0:T(8,128)} %filter_hbm.1, f32[1,256]{1,0:T(1,128)} %bitcast.1, bf16[2048,512]{1,0:T(8,128)(2,1)} %weight_hbm.1, ...), custom_call_target="tpu_custom_call" | custom-call | flops 2000000000 | bytes 5000000 | tf_op jit(solution)/shard_map/pallas_call | solution.py:377
  46.3 0.8 %copy.14 = bf16[512,512]{1,0:T(8,128)(2,1)} copy(bf16[512,512]{1,0:T(8,128)(2,1)S(1)} %shard_map.118) | data formatting | bytes 1048576

commit v3 on v2

--- a/solution.py
+++ b/solution.py
@@ -13,7 +13,7 @@
 LANES = 128
 F32 = jnp.float32
 BF16 = jnp.bfloat16
-RIGHTWARD, LEFTWARD_LAYER = (0,), 0
+RIGHTWARD, LEFTWARD_LAYERS = (1,), (0, 1)
 GRIDS = {32: (4, 4, 2), 8: (2, 2, 2), 4: (1, 2, 2)}
 
 
@@ -122,7 +122,7 @@
             stage[pl.ds(part * per + channel, seq, stride=block), :] = tile[channel * seq:(channel + 1) * seq, :]
 
     def staged():
-        return stage[...].astype(BF16).reshape(seq, block, LANES)
+        return stage[:rows, :].astype(BF16).reshape(seq, block, LANES)
 
     def send_all(source, target, slot):
         for other in others:
@@ -187,9 +187,9 @@
     loads[0].wait()
     prepare(0)
     pl.semaphore_wait(barrier, seq + 1)
-    for which in range(2):
-        send_all(send_in.at[0, which], recv_in.at[0, which], which)
+    send_all(send_in.at[0, 0], recv_in.at[0, 0], 0)
     send_all(send_edge, recv_edge, 2 * groups)
+    send_all(send_in.at[0, 1], recv_in.at[0, 1], 1)
     for group in range(1, groups):
         prepare(group)
         for which in range(2):
@@ -212,7 +212,7 @@
         return dot(high, table[0]) + dot(low, table[0]) + dot(high, table[1])
 
     def transform(group, which):
-        stage[...] = recv_in[group, which].reshape(rows, LANES).astype(F32)
+        stage[:rows, :] = recv_in[group, which].reshape(rows, LANES).astype(F32)
         if which == 1:
             first_lanes = lax.broadcasted_iota(jnp.int32, (seq, LANES), 1) < 2
             for channel in range(per):
@@ -220,16 +220,13 @@
                 place = (group * per + channel) * 8
                 whole = pltpu.roll(heads, (wide - place) % wide, 1)[:, :LANES]
                 stage[at, :] = jnp.where(first_lanes, whole, stage[at, :])
-        for pair in range(per // 2):
-            values = jnp.concatenate(
-                [stage[pl.ds(2 * pair + side, outer, stride=per), :] for side in range(2)], 1
-            ).astype(BF16)
-            outer_spec = dot(first[...], jnp.concatenate([values, values], 0))
-            for side in range(2):
-                real, imag = outer_spec[:outer, lanes(side)], outer_spec[outer:, lanes(side)]
-                at = slice((2 * pair + side) * outer, (2 * pair + side + 1) * outer)
-                high_ref[at, :LANES], low_ref[at, :LANES] = split(real * twist[0] + imag * twist[1])
-                high_ref[at, LANES:], low_ref[at, LANES:] = split(imag * twist[0] - real * twist[1])
+        values = jnp.concatenate([stage[pl.ds(channel, outer, stride=per), :] for channel in range(per)], 1).astype(BF16)
+        outer_spec = dot(first[...], jnp.concatenate([values, values], 0))
+        for channel in range(per):
+            real, imag = outer_spec[:outer, lanes(channel)], outer_spec[outer:, lanes(channel)]
+            at = slice(channel * outer, (channel + 1) * outer)
+            high_ref[at, :LANES], low_ref[at, :LANES] = split(real * twist[0] + imag * twist[1])
+            high_ref[at, LANES:], low_ref[at, LANES:] = split(imag * twist[0] - real * twist[1])
         spectrum[which * rows:(which + 1) * rows, :] = apply(forward)
 
     for group in range(groups):
@@ -259,7 +256,8 @@
                     [real * twist[0] - imag * twist[1], imag * twist[0] + real * twist[1]], 0
                 ))
             high, low = split(jnp.concatenate(sides, 1))
-            conv = dot(last[0], high) + dot(last[0], low) + dot(last[1], high)
+            both = dot(last[...].reshape(2 * outer, 2 * outer), high)
+            conv = both[:outer] + both[outer:] + dot(last[0], low)
             for side in range(2):
                 stage[pl.ds(2 * pair + side, outer, stride=per), :] = conv[:, lanes(side)]
         send_conv[group] = staged()
@@ -291,7 +289,8 @@
         if step < farthest - 1:
             act()
         elif group in RIGHTWARD:
-            pl.when(target != LEFTWARD_LAYER if direction == 0 else target == LEFTWARD_LAYER)(act)
+            by_left = functools.reduce(jnp.logical_or, [target == other for other in LEFTWARD_LAYERS])
+            pl.when(by_left if direction == 1 else jnp.logical_not(by_left))(act)
         elif direction == 1:
             act()
 
@@ -300,7 +299,7 @@
 
     for group in range(groups):
         wait_all(recv_conv.at[group], recv_sem.at[2 * groups + 1 + group])
-        stage[...] = recv_conv[group].reshape(rows, LANES).astype(F32)
+        stage[:rows, :] = recv_conv[group].reshape(rows, LANES).astype(F32)
         for part in range(sub):
             conv = jnp.concatenate(
                 [stage[pl.ds(part * per + channel, seq, stride=block), :] for channel in range(per)], 0
@@ -335,11 +334,8 @@
             if step == farthest:
                 for begin in (0, half):
                     at = slice(begin, begin + half)
-                    value = total[at, :] + product(origin_of(1, step), begin, half, (group,))
-                    if group < groups - 1:
-                        total[at, :] = value
-                    else:
-                        out_ref[at, :] = value.astype(BF16)
+                    if group == groups - 1:
+                        out_ref[at, :] = (total[at, :] + product(origin_of(1, step), begin, half)).astype(BF16)
         if step < farthest:
             for direction in (1, 0):
                 for begin in (0, half):
@@ -390,7 +386,7 @@
             pltpu.VMEM((3, tokens + 16, width), F32),
             pltpu.VMEM((tokens, width), F32),
             pltpu.VMEM((tokens, width), F32),
-            pltpu.VMEM((rows, LANES), F32),
+            pltpu.VMEM((rows + block, LANES), F32),
             pltpu.VMEM((wide, LANES), F32),
             edge, edge, incoming, incoming, returned, returned,
             pltpu.VMEM((2 * rows, 2 * LANES), F32),

time: 47.2 us -> 46.7 us (0.989)
  the two profiles are of different devices: /device:TPU:64 before, /device:TPU:1 now
where the time goes in v3:
time: 46.7 us; the launch traced here: 45.8 us
  Pallas kernels  45 us (96%)
  local copies, waits for them, and re-layouts  0.8 us (2%)
    pallas_call x1, Pallas kernels, shards(): pl.pallas_call(functools.partial(operator, GRIDS[seq], seq, chan), out_sh...  45 us

profile of v3, /device:TPU:1, one launch (start us, length us, event | category | flops | bytes accessed | tf_op | source)
XLA Modules:
  0.0 45.8 jit_solution(12833466501379542883)
XLA Ops:
  0.0 45.0 %shard_map.118 = bf16[512,512]{1,0:T(8,128)(2,1)S(1)} custom-call(bf16[512,256]{1,0:T(8,128)(2,1)} %query_hbm.1, bf16[512,256]{1,0:T(8,128)(2,1)} %key_hbm.1, bf16[512,256]{1,0:T(8,128)(2,1)} %value_hbm.1, f32[3,3,256]{2,1,0:T(4,128)} %taps_hbm.1, f32[512,256]{1,0:T(8,128)} %filter_hbm.1, f32[1,256]{1,0:T(1,128)} %bitcast.1, bf16[2048,512]{1,0:T(8,128)(2,1)} %weight_hbm.1, ...), custom_call_target="tpu_custom_call" | custom-call | flops 2000000000 | bytes 5000000 | tf_op jit(solution)/shard_map/pallas_call | solution.py:373
  45.0 0.8 %copy.14 = bf16[512,512]{1,0:T(8,128)(2,1)} copy(bf16[512,512]{1,0:T(8,128)(2,1)S(1)} %shard_map.118) | data formatting | bytes 1048576
